TPU v7x, 128 devices: a whole 4x4x4 slice. The times are simulated.
128 devices in a mesh: rep: 16 (over z, x_hi, core), sec: 2 (over x_lo), mdl: 4 (over y).
Axes of the slice: x: 4 (x_hi: 2, x_lo: 2; x = x_hi * 2 + x_lo), y: 4, z: 4, core: 2. Of those that a mesh axis runs over, the one named last changes fastest.
Arguments:
- obs: bfloat16 [2, 8192, 1536], P('sec', 'rep'), may hold values from -6 to 6
- a_query: bfloat16 [1536, 1536], P(None, 'mdl'), may hold values from -0.15309311 to 0.15309311
- a_keyval: bfloat16 [2, 1536, 512], P(None, None, 'mdl'), may hold values from -0.15309311 to 0.15309311
- a_out: bfloat16 [1536, 1536], P('mdl'), may hold values from -0.15625 to 0.15625
- w_policy: bfloat16 [1536, 128], replicated, may hold values from -0.15625 to 0.15625
- c_in: bfloat16 [1536, 2048], P(None, 'mdl'), may hold values from -0.15309311 to 0.15309311
- c_query: bfloat16 [2048, 2048], P(None, 'mdl'), may hold values from -0.13258252 to 0.13258252
- c_keyval: bfloat16 [2, 2048, 512], P(None, None, 'mdl'), may hold values from -0.13258252 to 0.13258252
- c_out: bfloat16 [2048, 2048], P('mdl'), may hold values from -0.125 to 0.125
- w_value: bfloat16 [2048], replicated, may hold values from -0.110485435 to 0.110485435
- actions: int32 [2, 8192], P('sec', 'rep'), may hold values from 0 to 127
- advantages: float32 [2, 8192], P('sec', 'rep'), may hold values from -6 to 6
- old_logp: float32 [2, 8192], P('sec', 'rep'), may hold values from -7 to -4
- returns: float32 [2, 8192], P('sec', 'rep'), may hold values from -6 to 6
- robot_count: int32 [2], replicated, may hold values from 2048 to 8192, as said below
Outputs:
- values: float32 [2, 8192], P('sec', ('rep', 'mdl'))
- grad_a_out: float32 [1536, 1536], P('mdl')
- grad_c_out: float32 [2048, 2048], P('mdl')
Inputs may be any that keep to these rules, and one draw needn't show every extreme that they name: `robot_count`: one of the two micro-batches holds all 8192 robots, the other at least 2048; live robots are the first ones.
All inputs are finite; a program needn't handle non-finite values.
Results may differ from a plain program's by a relative error of at most 0.023.
Values may be sent and summed in bfloat16 or wider, within the bound.
A program may use at most 128 MiB of HBM per device.

v0:
```python
import math
import jax
import jax.numpy as jnp
from jax import lax
from jax.sharding import PartitionSpec as P

HEAD = 128
epsilon = 1e-05
clip_range = 0.2
masked_score = -1e30


def rms_normed(values_in):
    return values_in * lax.rsqrt(jnp.mean(values_in * values_in, axis=-1, keepdims=True) + epsilon)


def norm_backward(source, normed, grad_in):
    factor = lax.rsqrt(jnp.mean(source * source, axis=-1, keepdims=True) + epsilon)
    return factor * (grad_in - normed * jnp.mean(grad_in * normed, axis=-1, keepdims=True))


def project(source, w_query, w_keyval):
    normed = rms_normed(source).astype(jnp.bfloat16)
    queries = (
        jnp.dot(normed, w_query, preferred_element_type=jnp.float32) * HEAD ** (-0.5)
    ).astype(jnp.bfloat16)
    keyval = jnp.einsum("rd,cdk->crk", normed, w_keyval, preferred_element_type=jnp.float32).astype(
        jnp.bfloat16
    )
    return (queries, keyval)


def policy_backward(hidden, action_ids, advantage, old_values, live_mask, live_total, w_policy):
    source = hidden.astype(jnp.float32)
    normed = rms_normed(source)
    logits = jnp.dot(normed.astype(jnp.bfloat16), w_policy, preferred_element_type=jnp.float32)
    log_probs = jax.nn.log_softmax(logits, axis=-1)
    onehot = (action_ids[:, None] == lax.broadcasted_iota(jnp.int32, logits.shape, 1)).astype(
        jnp.float32
    )
    chosen = jnp.sum(onehot * log_probs, axis=-1)
    prob_ratio = jnp.exp(chosen - old_values)
    plain_term = prob_ratio * advantage
    bounded = jnp.clip(prob_ratio, 1.0 - clip_range, 1.0 + clip_range) * advantage
    slope_term = jnp.where(
        live_mask & (plain_term <= bounded), -plain_term / live_total, jnp.float32(0.0)
    )
    dlogits = slope_term[:, None] * (onehot - jnp.exp(log_probs))
    dnormed = jnp.dot(dlogits, w_policy.astype(jnp.float32).T, precision=lax.Precision.HIGHEST)
    return norm_backward(source, normed, dnormed)


def value_backward(mixed_out, target, live_mask, live_total, w_value):
    normed = rms_normed(mixed_out)
    value_pred = jnp.dot(normed.astype(jnp.bfloat16), w_value, preferred_element_type=jnp.float32)
    slope_term = jnp.where(live_mask, value_pred - target, jnp.float32(0.0)) / live_total
    dnormed = slope_term[:, None] * w_value.astype(jnp.float32)[None, :]
    return (value_pred, norm_backward(mixed_out, normed, dnormed))


def split_heads(queries, kv_heads):
    row_count = queries.shape[0]
    groups = queries.shape[1] // HEAD // kv_heads
    return queries.reshape(row_count, kv_heads, groups, HEAD)


def start_state(heads_in):
    row_count, kv_heads, groups, _ = heads_in.shape
    row_top = jnp.full((kv_heads, groups, row_count), masked_score, jnp.float32)
    row_sum = jnp.zeros((kv_heads, groups, row_count), jnp.float32)
    acc_sum = jnp.zeros((kv_heads, groups, row_count, HEAD), jnp.float32)
    return (row_top, row_sum, acc_sum)


def make_fold(heads_in, robot_total, carried, piece):
    kv_heads = heads_in.shape[1]
    piece_rows = piece.shape[1]
    block_rows = math.gcd(piece_rows, 512)
    block_count = piece_rows // block_rows
    key_blocks = piece[0].reshape(block_count, block_rows, kv_heads, HEAD)
    value_blocks = piece[1].reshape(block_count, block_rows, kv_heads, HEAD)

    def absorb(inner, block_item):
        block_index, key_block, value_block = block_item
        first_key = block_index * block_rows
        row_top, row_sum, acc_sum = inner
        scores = jnp.einsum(
            "rkgd,jkd->kgrj", heads_in, key_block, preferred_element_type=jnp.float32
        )
        key_live = first_key + lax.iota(jnp.int32, block_rows) < robot_total
        scores = jnp.where(key_live, scores, masked_score)
        new_top = jnp.maximum(row_top, jnp.max(scores, axis=-1))
        rescale = jnp.exp(row_top - new_top)
        weights = jnp.exp(scores - new_top[..., None])
        row_sum = row_sum * rescale + jnp.sum(weights, axis=-1)
        value_float = value_block.astype(jnp.float32)
        acc_sum = acc_sum * rescale[..., None] + jnp.einsum(
            "kgrj,jkd->kgrd", weights, value_float, precision=lax.Precision.HIGHEST
        )
        return ((new_top, row_sum, acc_sum), None)

    result, _ = lax.scan(
        absorb, carried, (jnp.arange(block_count, dtype=jnp.int32), key_blocks, value_blocks)
    )
    return result


def finish_heads(carried):
    _, row_sum, acc_sum = carried
    combined = acc_sum / row_sum[..., None]
    kv_heads, groups, row_count, _ = combined.shape
    return (
        jnp.transpose(combined, (2, 0, 1, 3))
        .reshape(row_count, kv_heads * groups * HEAD)
        .astype(jnp.bfloat16)
    )


def on_device(
    obs,
    a_query,
    a_keyval,
    a_out,
    w_policy,
    c_in,
    c_query,
    c_keyval,
    c_out,
    w_value,
    actions,
    advantages,
    old_logp,
    returns,
    robot_count,
):
    row_count = obs.shape[1]
    batch_index = lax.axis_index("sec")
    robot_total = robot_count[batch_index]
    live_total = jnp.sum(robot_count).astype(jnp.float32)
    first_row = lax.axis_index("rep") * row_count
    live_mask = first_row + lax.iota(jnp.int32, row_count) < robot_total
    mdl_count = lax.axis_size("mdl")
    part_rows = row_count // mdl_count
    row_start = lax.axis_index("mdl") * part_rows
    obs_float = obs[0].astype(jnp.float32)
    queries, keyval = project(obs_float, a_query, a_keyval)
    heads_a = split_heads(queries, keyval.shape[2] // HEAD)
    state_a = make_fold(
        heads_a,
        robot_total,
        start_state(heads_a),
        lax.all_gather(keyval, "rep", axis=1, tiled=True),
    )
    attended = finish_heads(state_a)
    mixed_sum = lax.psum(jnp.dot(attended, a_out, preferred_element_type=jnp.float32), "mdl")
    hidden = (obs_float + mixed_sum).astype(jnp.bfloat16)
    dhidden = policy_backward(
        hidden, actions[0], advantages[0], old_logp[0], live_mask, live_total, w_policy
    ).astype(jnp.bfloat16)
    actor_grad = jnp.einsum("rh,rd->hd", attended, dhidden, preferred_element_type=jnp.float32)
    embed_part = jnp.dot(hidden, c_in, preferred_element_type=jnp.float32).astype(jnp.bfloat16)
    embedded = lax.all_gather(embed_part, "mdl", axis=1, tiled=True)
    embed_float = embedded.astype(jnp.float32)
    critic_queries, critic_keyval = project(embed_float, c_query, c_keyval)
    heads_c = split_heads(critic_queries, critic_keyval.shape[2] // HEAD)
    state_c = make_fold(
        heads_c,
        robot_total,
        start_state(heads_c),
        lax.all_gather(critic_keyval, "rep", axis=1, tiled=True),
    )
    critic_attended = finish_heads(state_c)
    critic_sum = lax.psum(
        jnp.dot(critic_attended, c_out, preferred_element_type=jnp.float32).astype(jnp.bfloat16),
        "mdl",
    ).astype(jnp.float32)
    value_pred, dmixed = value_backward(
        embed_float + critic_sum, returns[0], live_mask, live_total, w_value
    )
    value_part = lax.dynamic_slice_in_dim(value_pred, row_start, part_rows, 0)
    dmixed_all = dmixed.astype(jnp.bfloat16)
    critic_grad = jnp.einsum(
        "rh,rd->hd", critic_attended, dmixed_all, preferred_element_type=jnp.float32
    )
    actor_summed, critic_summed = (
        lax.psum(actor_grad.astype(jnp.bfloat16), ("rep", "sec")).astype(jnp.float32),
        lax.psum(critic_grad.astype(jnp.bfloat16), ("rep", "sec")).astype(jnp.float32),
    )
    return (value_part[None, :], actor_summed, critic_summed)


def solution(mesh):
    return jax.shard_map(
        on_device,
        mesh=mesh,
        in_specs=(
            P("sec", "rep", None),
            P(None, "mdl"),
            P(None, None, "mdl"),
            P("mdl", None),
            P(),
            P(None, "mdl"),
            P(None, "mdl"),
            P(None, None, "mdl"),
            P("mdl", None),
            P(),
            P("sec", "rep"),
            P("sec", "rep"),
            P("sec", "rep"),
            P("sec", "rep"),
            P(),
        ),
        out_specs=(P("sec", ("rep", "mdl")), P("mdl", None), P("mdl", None)),
        check_vma=False,
    )
```

profile of v0, /device:TPU:1, one launch (start us, length us, event | category | flops | bytes accessed | tf_op | source)
XLA Modules:
  0.0 878.9 jit_solution(12537995733930431458)
XLA Ops:
  17.4 53.9 %all-gather.4.cloned.1.call-done = bf16[2,8192,128]{2,1,0:T(8,128)(2,1)} async-done(((bf16[2,512,128]{2,1,0:T(8,128)(2,1)}), bf16[2,8192,128]{2,1,0:T(8,128)(2,1)}) %all-gather.4.cloned.1.call-update) | async-done | bytes 4194320 | tf_op jit(solution)/shard_map/all_gather | solution.py:152
  71.4 4.5 fusion.116
  75.9 188.8 %while.30 = (s32[]{:T(128)}, f32[1,3,512]{2,1,0:T(4,128)S(1)}, f32[1,3,512]{2,1,0:T(4,128)S(1)}, f32[1,3,512,128]{3,2,1,0:T(8,128)S(1)}, s32[16]{0:T(128)S(1)}, ...) while((s32[]{:T(128)}, f32[1,3,512]{2,1,0:T(4,128)S(1)}, ...), condition=%wide.region_4.5_spmd.clone, body=%wide.region_1.4_spmd.clone.sunk | while | flops 1415391232 | bytes 24348876 | solution.py:102
  95.5 3.9 fusion.148
  107.3 3.9 fusion.148
  119.1 3.9 fusion.148
  130.9 3.9 fusion.148
  267.0 3.9 fusion.118
  271.0 73.2 %all-reduce.5.cloned.1.call-done = f32[512,1536]{1,0:T(8,128)} async-done(((f32[512,1536]{1,0:T(8,128)}), f32[512,1536]{1,0:T(8,128)}) %all-reduce.5.cloned.1.call-update) | async-done | bytes 3145744 | tf_op jit(solution)/shard_map/psum | solution.py:155
  350.9 30.8 %all-gather.6.cloned.1.call-done = bf16[512,2048]{1,0:T(8,128)(2,1)} async-done(((bf16[512,512]{1,0:T(8,128)(2,1)}), bf16[512,2048]{1,0:T(8,128)(2,1)}) %all-gather.6.cloned.1.call-update) | async-done | bytes 2097168 | tf_op jit(solution)/shard_map/all_gather | solution.py:162
  387.1 4.4 fusion.84
  393.5 49.4 %all-gather.8.cloned.1.call-done = bf16[2,8192,128]{2,1,0:T(8,128)(2,1)} async-done(((bf16[2,512,128]{2,1,0:T(8,128)(2,1)}), bf16[2,8192,128]{2,1,0:T(8,128)(2,1)}) %all-gather.8.cloned.1.call-update) | async-done | bytes 4194320 | tf_op jit(solution)/shard_map/all_gather | solution.py:170
  442.8 4.5 fusion.115
  447.4 234.7 %while.31 = (s32[]{:T(128)}, f32[1,4,512]{2,1,0:T(4,128)S(1)}, f32[1,4,512]{2,1,0:T(4,128)}, f32[1,4,512,128]{3,2,1,0:T(8,128)S(1)}, s32[16]{0:T(128)S(1)}, /*in...) while((s32[]{:T(128)}, f32[1,4,512]{2,1,0:T(4,128)S(1)}, ...), condition=%wide.region_10.11_spmd.clone, body=%wide.region_7.10_spmd.clone.sunk | while | flops 1887187968 | bytes 32447348 | solution.py:102
  457.1 4.9 fusion.153
  471.7 4.9 fusion.153
  486.4 4.9 fusion.153
  501.1 4.9 fusion.153
  515.7 4.9 fusion.153
  530.4 4.9 fusion.153
  545.1 4.9 fusion.153
  559.7 4.9 fusion.153
  574.4 4.9 fusion.153
  589.1 4.9 fusion.153
  603.8 4.9 fusion.153
  618.4 4.9 fusion.153
  633.1 4.9 fusion.153
  647.8 4.9 fusion.153
  662.4 4.9 fusion.153
  677.1 4.9 fusion.153
  691.4 52.2 %all-reduce.7.cloned.1.call-done = bf16[512,2048]{1,0:T(8,128)(2,1)} async-done(((bf16[512,2048]{1,0:T(8,128)(2,1)}), bf16[512,2048]{1,0:T(8,128)(2,1)}) %all-reduce.7.cloned.1.call-update) | async-done | bytes 2097168 | tf_op jit(solution)/shard_map/psum | solution.py:173
  757.4 109.0 %all-reduce.9.cloned.1.call-done = (bf16[384,1536]{1,0:T(8,128)(2,1)}, bf16[512,2048]{1,0:T(8,128)(2,1)}) async-done(((bf16[384,1536]{1,0:T(8,128)(2,1)}, bf16[512,2048]{1,0:T(8,128)(2,1)}), (bf16[384,1536]{1,0:T(8,128)(2,1)}, bf16[512,2048]{1,0:T(8,128)(2,1)})) %all-reduce.9.cloned.1.call-update) | async-done | bytes 3276816 | tf_op jit(solution)/shard_map/psum | solution.py:186
  (584 shorter events, 359.9 us)
Async XLA Ops:
  7.2 677.6 %copy-start = (bf16[512,2048]{1,0:T(8,128)(2,1)S(1)}, bf16[512,2048]{1,0:T(8,128)(2,1)}, u32[]{:S(2)}) copy-start(bf16[512,2048]{1,0:T(8,128)(2,1)} %param.27) | copy-start | bytes 6291460
  7.2 64.2 %all-gather.4.cloned.1.call-start = ((), (), s32[]{:S(2)}) async-start(), calls=%async_computation | async-start | bytes 4456448 | tf_op jit(solution)/shard_map/all_gather | solution.py:152
  12.1 332.1 %all-reduce.5.cloned.1.call-start = ((), (), s32[]{:S(2)}) async-start(), calls=%async_computation.1 | async-start | bytes 6291456 | tf_op jit(solution)/shard_map/psum | solution.py:155
  271.0 110.7 %all-gather.6.cloned.1.call-start = ((), (), s32[]{:S(2)}) async-start(), calls=%async_computation.2 | async-start | bytes 2621440 | tf_op jit(solution)/shard_map/all_gather | solution.py:162
  349.0 34.7 %copy-start.20 = (bf16[2,2048,128]{2,1,0:T(8,128)(2,1)S(1)}, bf16[2,2048,128]{2,1,0:T(8,128)(2,1)}, u32[]{:S(2)}) copy-start(bf16[2,2048,128]{2,1,0:T(8,128)(2,1)} %param.26) | copy-start | bytes 3145732
  350.8 92.0 %all-gather.8.cloned.1.call-start = ((), (), s32[]{:S(2)}) async-start(), calls=%async_computation.3 | async-start | bytes 4456448 | tf_op jit(solution)/shard_map/all_gather | solution.py:170
  386.8 356.8 %all-reduce.7.cloned.1.call-start = ((), (), s32[]{:S(2)}) async-start(), calls=%async_computation.4 | async-start | bytes 4194304 | tf_op jit(solution)/shard_map/psum | solution.py:173
  456.8 5.2 copy-start.10
  457.1 5.0 copy-start.24
  471.4 5.2 copy-start.10
  486.1 5.2 copy-start.10
  486.4 5.0 copy-start.24
  500.8 5.2 copy-start.10
  501.1 5.0 copy-start.24
  515.5 5.2 copy-start.10
  515.7 5.0 copy-start.24
  530.1 5.2 copy-start.10
  544.8 5.2 copy-start.10
  545.1 5.0 copy-start.24
  559.5 5.2 copy-start.10
  559.7 5.0 copy-start.24
  574.1 5.2 copy-start.10
  574.4 5.0 copy-start.24
  588.8 5.2 copy-start.10
  603.5 5.2 copy-start.10
  618.1 5.2 copy-start.10
  632.8 5.2 copy-start.10
  647.5 5.2 copy-start.10
  662.2 5.2 copy-start.10
  662.4 5.0 copy-start.24
  676.8 5.2 copy-start.10
  687.4 179.0 %all-reduce.9.cloned.1.call-start = ((), (), s32[]{:S(2)}) async-start(), calls=%async_computation.5 | async-start | bytes 6553600 | tf_op jit(solution)/shard_map/psum | solution.py:186
  (119 other events, 327.2 us)
Sparse Core Ops, SparseCore 0:
  12.2 59.0 all-gather.3
  271.1 73.0 all-reduce.4
  350.9 30.6 all-gather.5
  386.9 55.8 all-gather.7
  687.5 56.0 all-reduce.6
  756.9 109.4 all-reduce.8
where the time goes:
time: 881 us; the launch traced here: 879 us
  waiting for transfers between devices  369 us (42%)
  matrix products  286 us (32%)
  other arithmetic  135 us (15%)
  local copies, waits for them, and re-layouts  50.4 us (6%)
  loops' own time  23.5 us (3%)
  between operations  15.1 us (2%)
    dot_general x32, matrix products, absorb(): jnp.einsum('kgrj,jkd->kgrd', weights, value_float, precision=lax.Precisio...  142 us
    dot_general x32, matrix products, absorb(): jnp.einsum('rkgd,jkd->kgrj', heads_in, key_block, preferred_element_type=...  112 us
    psum x1, waiting for transfers between devices, on_device(): lax.psum(actor_grad.astype(jnp.bfloat16), ('rep', 'sec'))  109 us
    reduce_sum x32, other arithmetic, absorb(): row_sum = row_sum * rescale + jnp.sum(weights, axis=-1)  92.6 us
    psum x1, waiting for transfers between devices, on_device(): lax.psum(jnp.dot(attended, a_out, preferred_element_type=jnp.float32), 'm...  73.2 us
    all_gather x1, waiting for transfers between devices, on_device(): lax.all_gather(keyval, 'rep', axis=1, tiled=True)  53.9 us
    psum x1, waiting for transfers between devices, on_device(): lax.psum(jnp.dot(critic_attended, c_out, preferred_element_type=jnp.float...  52.2 us
    all_gather x1, waiting for transfers between devices, on_device(): lax.all_gather(critic_keyval, 'rep', axis=1, tiled=True)  49.4 us
  transfers between devices with their start and end apart: 6, of which 6 were waited for; matrix products, arithmetic and copies ran while one was open for 2% of the time, Pallas kernels for 0%

commit v1 on v0

--- a/solution.py
+++ b/solution.py
@@ -183,7 +183,7 @@
         "rh,rd->hd", critic_attended, dmixed_all, preferred_element_type=jnp.float32
     )
     actor_summed, critic_summed = (
-        lax.psum(actor_grad.astype(jnp.bfloat16), ("rep", "sec")).astype(jnp.float32),
+        lax.psum(lax.psum(actor_grad.astype(jnp.bfloat16), "rep"), "sec").astype(jnp.float32),
         lax.psum(critic_grad.astype(jnp.bfloat16), ("rep", "sec")).astype(jnp.float32),
     )
     return (value_part[None, :], actor_summed, critic_summed)

time: 881 us -> 876 us (level)
  other arithmetic: 135 us -> 69.1 us
  matrix products: 286 us -> 327 us
  waiting for transfers between devices: 369 us -> 403 us
  local copies, waits for them, and re-layouts: 50.4 us -> 37.1 us
    reduce_sum x32, other arithmetic: 92.6 us -> 22.1 us  [absorb(): row_sum = row_sum * rescale + jnp.sum(weights, axis=-1)]
    psum x1 -> x3, waiting for transfers between devices: 109 us -> 152 us  [the longest x1 109 us: on_device(): lax.psum(critic_grad.astype(jnp.bfloat16), ('rep', 'sec'))]
    dot_general x32, matrix products: 142 us -> 182 us  [absorb(): jnp.einsum('kgrj,jkd->kgrd', weights, value_float, precision=lax.Precisio...]
    while x288 -> x96, local copies, waits for them, and re-layouts: 14.1 us -> 0.25 us
    all_gather x1, waiting for transfers between devices: 49.4 us -> 37.3 us  [on_device(): lax.all_gather(critic_keyval, 'rep', axis=1, tiled=True)]
  transfers between devices with their start and end apart: 6 -> 8, of which waited for: 6 -> 7; matrix products, arithmetic and copies ran while one was open for 2% -> 27% of each run, Pallas kernels for 0% -> 0%
where the time goes in v1:
time: 876 us; the launch traced here: 874 us
  waiting for transfers between devices  403 us (46%)
  matrix products  327 us (37%)
  other arithmetic  69.1 us (8%)
  local copies, waits for them, and re-layouts  37.1 us (4%)
  loops' own time  22.7 us (3%)
  between operations  15 us (2%)
    dot_general x32, matrix products, absorb(): jnp.einsum('kgrj,jkd->kgrd', weights, value_float, precision=lax.Precisio...  182 us
    dot_general x32, matrix products, absorb(): jnp.einsum('rkgd,jkd->kgrj', heads_in, key_block, preferred_element_type=...  112 us
    psum x1, waiting for transfers between devices, on_device(): lax.psum(critic_grad.astype(jnp.bfloat16), ('rep', 'sec'))  109 us
    psum x1, waiting for transfers between devices, on_device(): lax.psum(jnp.dot(attended, a_out, preferred_element_type=jnp.float32), 'm...  73.2 us
    psum x1, waiting for transfers between devices, on_device(): lax.psum(jnp.dot(critic_attended, c_out, preferred_element_type=jnp.float...  55.3 us
    all_gather x1, waiting for transfers between devices, on_device(): lax.all_gather(keyval, 'rep', axis=1, tiled=True)  53.9 us
    psum x1, waiting for transfers between devices, on_device(): lax.psum(lax.psum(actor_grad.astype(jnp.bfloat16), 'rep'), 'sec')  42.8 us
    all_gather x1, waiting for transfers between devices, on_device(): lax.all_gather(critic_keyval, 'rep', axis=1, tiled=True)  37.3 us
  transfers between devices with their start and end apart: 8, of which 7 were waited for; matrix products, arithmetic and copies ran while one was open for 27% of the time, Pallas kernels for 0%

profile of v1, /device:TPU:1, one launch (start us, length us, event | category | flops | bytes accessed | tf_op | source)
XLA Modules:
  0.0 874.4 jit_solution(1754287841930516157)
XLA Ops:
  17.5 53.9 %all-gather.4.cloned.1.call-done = bf16[2,8192,128]{2,1,0:T(8,128)(2,1)} async-done(((bf16[2,512,128]{2,1,0:T(8,128)(2,1)}), bf16[2,8192,128]{2,1,0:T(8,128)(2,1)}) %all-gather.4.cloned.1.call-update) | async-done | bytes 4194320 | tf_op jit(solution)/shard_map/all_gather | solution.py:152
  75.9 171.9 %while.30 = (s32[]{:T(128)}, f32[1,3,512]{2,1,0:T(4,128)S(1)}, f32[1,3,512]{2,1,0:T(4,128)S(1)}, f32[1,3,512,128]{3,2,1,0:T(8,128)S(1)}, s32[16]{0:T(128)S(1)}, ...) while((s32[]{:T(128)}, f32[1,3,512]{2,1,0:T(4,128)S(1)}, ...), condition=%wide.region_4.5_spmd.clone, body=%wide.region_1.4_spmd.clone.sunk | while | flops 1415391232 | bytes 24349884 | solution.py:102
  80.9 5.0 fusion.148
  91.6 5.0 fusion.148
  102.4 5.0 fusion.148
  113.1 5.0 fusion.148
  123.9 5.0 fusion.148
  166.9 5.0 fusion.148
  209.8 5.0 fusion.148
  254.2 73.2 %all-reduce.6.cloned.1.call-done = f32[512,1536]{1,0:T(8,128)} async-done(((f32[512,1536]{1,0:T(8,128)}), f32[512,1536]{1,0:T(8,128)}) %all-reduce.6.cloned.1.call-update) | async-done | bytes 3145744 | tf_op jit(solution)/shard_map/psum | solution.py:155
  334.0 30.8 %all-gather.6.cloned.1.call-done = bf16[512,2048]{1,0:T(8,128)(2,1)} async-done(((bf16[512,512]{1,0:T(8,128)(2,1)}), bf16[512,2048]{1,0:T(8,128)(2,1)}) %all-gather.6.cloned.1.call-update) | async-done | bytes 2097168 | tf_op jit(solution)/shard_map/all_gather | solution.py:162
  389.3 37.3 %all-gather.8.cloned.1.call-done = bf16[2,8192,128]{2,1,0:T(8,128)(2,1)} async-done(((bf16[2,512,128]{2,1,0:T(8,128)(2,1)}), bf16[2,8192,128]{2,1,0:T(8,128)(2,1)}) %all-gather.8.cloned.1.call-update) | async-done | bytes 4194320 | tf_op jit(solution)/shard_map/all_gather | solution.py:170
  431.1 206.6 %while.31 = (s32[]{:T(128)}, f32[1,4,512]{2,1,0:T(4,128)S(1)}, f32[1,4,512]{2,1,0:T(4,128)S(1)}, f32[1,4,512,128]{3,2,1,0:T(8,128)S(1)}, s32[16]{0:T(128)S(1)}, ...) while((s32[]{:T(128)}, f32[1,4,512]{2,1,0:T(4,128)S(1)}, ...), condition=%wide.region_10.11_spmd.clone, body=%wide.region_7.10_spmd.clone.sunk | while | flops 1887187968 | bytes 32378044 | solution.py:102
  436.8 6.3 fusion.153
  449.7 6.3 fusion.153
  462.6 6.3 fusion.153
  475.5 6.4 fusion.153
  488.5 6.3 fusion.153
  501.4 6.3 fusion.153
  514.3 6.3 fusion.153
  527.2 6.3 fusion.153
  540.1 6.3 fusion.153
  553.0 6.3 fusion.153
  565.9 6.3 fusion.153
  578.8 6.3 fusion.153
  591.8 6.3 fusion.153
  604.7 6.3 fusion.153
  617.6 6.3 fusion.153
  630.5 6.3 fusion.153
  644.0 55.3 %all-reduce.8.cloned.1.call-done = bf16[512,2048]{1,0:T(8,128)(2,1)} async-done(((bf16[512,2048]{1,0:T(8,128)(2,1)}), bf16[512,2048]{1,0:T(8,128)(2,1)}) %all-reduce.8.cloned.1.call-update) | async-done | bytes 2097168 | tf_op jit(solution)/shard_map/psum | solution.py:173
  708.4 42.8 %all-reduce.12.cloned.1.call-done = bf16[384,1536]{1,0:T(8,128)(2,1)} async-done(((bf16[384,1536]{1,0:T(8,128)(2,1)}), bf16[384,1536]{1,0:T(8,128)(2,1)}) %all-reduce.12.cloned.1.call-update) | async-done | bytes 1179664 | tf_op jit(solution)/shard_map/psum | solution.py:186
  754.7 108.8 %all-reduce.14.cloned.1.call-done = bf16[512,2048]{1,0:T(8,128)(2,1)} async-done(((bf16[512,2048]{1,0:T(8,128)(2,1)}), bf16[512,2048]{1,0:T(8,128)(2,1)}) %all-reduce.14.cloned.1.call-update) | async-done | bytes 2097168 | tf_op jit(solution)/shard_map/psum | solution.py:187
  (389 shorter events, 298.1 us)
Async XLA Ops:
  7.2 633.2 %copy-start = (bf16[512,2048]{1,0:T(8,128)(2,1)S(1)}, bf16[512,2048]{1,0:T(8,128)(2,1)}, u32[]{:S(2)}) copy-start(bf16[512,2048]{1,0:T(8,128)(2,1)} %param.27) | copy-start | bytes 6291460
  7.2 64.2 %all-gather.4.cloned.1.call-start = ((), (), s32[]{:S(2)}) async-start(), calls=%async_computation | async-start | bytes 4456448 | tf_op jit(solution)/shard_map/all_gather | solution.py:152
  12.1 315.3 %all-reduce.6.cloned.1.call-start = ((), (), s32[]{:S(2)}) async-start(), calls=%async_computation.1 | async-start | bytes 6291456 | tf_op jit(solution)/shard_map/psum | solution.py:155
  80.9 5.1 copy-start.2
  123.9 5.1 copy-start.2
  166.8 5.1 copy-start.2
  209.8 5.1 copy-start.2
  254.1 110.6 %all-gather.6.cloned.1.call-start = ((), (), s32[]{:S(2)}) async-start(), calls=%async_computation.2 | async-start | bytes 2621440 | tf_op jit(solution)/shard_map/all_gather | solution.py:162
  332.1 35.3 %copy-start.12 = (bf16[2,2048,128]{2,1,0:T(8,128)(2,1)S(1)}, bf16[2,2048,128]{2,1,0:T(8,128)(2,1)}, u32[]{:S(2)}) copy-start(bf16[2,2048,128]{2,1,0:T(8,128)(2,1)} %param.26) | copy-start | bytes 3145732
  333.9 92.6 %all-gather.8.cloned.1.call-start = ((), (), s32[]{:S(2)}) async-start(), calls=%async_computation.3 | async-start | bytes 4456448 | tf_op jit(solution)/shard_map/all_gather | solution.py:170
  370.5 272.6 %all-reduce.10.cloned.1.call-start = ((), (), s32[]{:S(2)}) async-start(), calls=%async_computation.5 | async-start | bytes 2359296 | tf_op jit(solution)/shard_map/psum | solution.py:186
  372.8 5.2 copy-start.5
  372.8 5.2 copy-start.7
  382.8 316.5 %all-reduce.8.cloned.1.call-start = ((), (), s32[]{:S(2)}) async-start(), calls=%async_computation.4 | async-start | bytes 4194304 | tf_op jit(solution)/shard_map/psum | solution.py:173
  436.8 6.4 copy-start.1
  449.7 6.4 copy-start.1
  462.6 6.4 copy-start.1
  475.5 6.4 copy-start.1
  488.5 6.4 copy-start.1
  501.4 6.4 copy-start.1
  514.3 6.4 copy-start.1
  527.2 6.4 copy-start.1
  540.1 6.4 copy-start.1
  553.0 6.4 copy-start.1
  565.9 6.4 copy-start.1
  578.8 6.4 copy-start.1
  591.7 6.4 copy-start.1
  604.7 6.4 copy-start.1
  617.6 6.4 copy-start.1
  630.5 6.4 copy-start.1
  643.0 108.2 %all-reduce.12.cloned.1.call-start = ((), (), s32[]{:S(2)}) async-start(), calls=%async_computation.6 | async-start | bytes 2359296 | tf_op jit(solution)/shard_map/psum | solution.py:186
  643.7 219.7 %all-reduce.14.cloned.1.call-start = ((), (), s32[]{:S(2)}) async-start(), calls=%async_computation.7 | async-start | bytes 4194304 | tf_op jit(solution)/shard_map/psum | solution.py:187
  (20 other events, 82.6 us)
Sparse Core Ops, SparseCore 0:
  12.2 59.0 all-gather.3
  254.2 73.0 all-reduce.5
  334.0 30.6 all-gather.5
  370.6 55.8 all-gather.7
  428.9 138.5 all-reduce.9
  643.1 56.1 all-reduce.7
  701.8 49.2 all-reduce.11
  755.0 108.4 all-reduce.13
